TPU v7x, 512 devices: a whole 4x4x16 slice. The times are simulated.
512 devices in a mesh: vox: 64 (over y, z_lo, core), mode: 8 (over z_hi, x).
Axes of the slice: x: 4, y: 4, z: 16 (z_hi: 2, z_lo: 8; z = z_hi * 8 + z_lo), core: 2. Of those that a mesh axis runs over, the one named last changes fastest.
Arguments:
- modes_in: bfloat16 [128, 3, 64, 32, 128], P('mode', None, 'vox'), may hold values from -6 to 6
- class_map: int32 [64, 32, 128], P('vox'), may hold values from 0 to 7
- stiffness_table: float32 [8], replicated, may hold values from 0.5 to 2
- coefficients: float32 [128, 128], replicated, may hold values from -0.5 to 0.5
Outputs:
- modes_out: bfloat16 [128, 3, 64, 32, 128], P('mode', None, 'vox')
Inputs may be any that keep to these rules, and one draw needn't show every extreme that they name: `class_map`: class numbers index the stiffness table.
All inputs are finite; a program needn't handle non-finite values.
Results may differ from a plain program's by a relative error of at most 0.0081.
Values may be sent and summed in bfloat16 or wider, within the bound.
A program may use at most 64 MiB of HBM per device.

v0:
```python
import jax
import jax.numpy as jnp
from jax import lax
from jax.sharding import PartitionSpec as P

DEGREE = 3


def with_halo(x, sides, width):
    for axis, dim in sides:
        count, length = (lax.axis_size(axis), x.shape[dim])
        up = [(i, (i + 1) % count) for i in range(count)]
        down = [(j, i) for i, j in up]
        last = lax.slice_in_dim(x, length - width, length, axis=dim)
        leading = lax.slice_in_dim(x, 0, width, axis=dim)
        before = lax.ppermute(last, axis, up)
        after = lax.ppermute(leading, axis, down)
        x = jnp.concatenate([before, x, after], axis=dim)
    return x


def offset_list():
    found = []
    for dz in (-1, 0, 1):
        for dx in (-1, 0, 1):
            for dy in (-1, 0, 1):
                count = abs(dz) + abs(dx) + abs(dy)
                if count > 0:
                    found.append((dz, dx, dy, [0.0, 1.0, 0.5, 0.25][count]))
    return found


def pad_plane(field):
    lead = field.ndim - 2
    return jnp.pad(field, [(0, 0)] * lead + [(1, 1), (1, 1)])


def shifted(padded, dz, dx, dy, zlen, xlen, ylen):
    return padded[..., 1 + dz : 1 + dz + zlen, 1 + dx : 1 + dx + xlen, 1 + dy : 1 + dy + ylen]


def make_mix(gram, coefficients, total_rows):
    lower = jnp.linalg.cholesky(gram)
    solved = lax.linalg.triangular_solve(
        lower, coefficients, left_side=True, lower=True, transpose_a=True
    )
    return (solved * jnp.sqrt(jnp.float32(total_rows))).astype(jnp.bfloat16)


def gram_local(flat):
    return lax.dot_general(flat, flat, (((1,), (1,)), ((), ())), preferred_element_type=jnp.float32)


def per_device(modes_in, class_map, stiffness_table, coefficients):
    mode_block, comps, zlen, xlen, ylen = modes_in.shape
    classes = jnp.arange(stiffness_table.shape[0], dtype=jnp.int32)
    stiff = jnp.sum(
        jnp.where(
            class_map[None] == classes[:, None, None, None],
            stiffness_table[:, None, None, None],
            jnp.float32(0.0),
        ),
        axis=0,
    )
    srim = with_halo(stiff, (("vox", 0),), 1)
    spad = pad_plane(srim)
    terms = []
    for dz, dx, dy, weight in offset_list():
        terms.append(
            (dz, dx, dy, weight * 0.5 * (stiff + shifted(spad, dz, dx, dy, zlen, xlen, ylen)))
        )

    def apply_op(field):
        rimmed = with_halo(field, (("vox", 2),), 1)
        padded = pad_plane(rimmed)
        total = jnp.zeros_like(field)
        for dz, dx, dy, kedge in terms:
            total = total + kedge * (field - shifted(padded, dz, dx, dy, zlen, xlen, ylen))
        return total

    scale_e = jnp.float32(21.0)
    centre = jnp.float32(35.0)
    older = modes_in.astype(jnp.float32)
    newer = (apply_op(older) - centre * older) / scale_e
    for step in range(DEGREE - 1):
        nxt = 2.0 * (apply_op(newer) - centre * newer) / scale_e - older
        older, newer = (newer, nxt)
    filtered = newer.astype(jnp.bfloat16)
    total_rows = comps * zlen * xlen * ylen * lax.axis_size("vox")
    every_mode = lax.all_gather(filtered, "mode", axis=0, tiled=True)
    flat = every_mode.reshape(every_mode.shape[0], -1)
    gram = lax.psum(gram_local(flat), "vox")
    mix = make_mix(gram, coefficients, total_rows)
    start = lax.axis_index("mode") * mode_block
    own_cols = lax.dynamic_slice_in_dim(mix, start, mode_block, 1)
    result = lax.dot_general(
        own_cols, flat, (((0,), (0,)), ((), ())), preferred_element_type=jnp.float32
    )
    return result.astype(jnp.bfloat16).reshape(modes_in.shape)


def solution(mesh):
    in_specs = (P("mode", None, "vox", None, None), P("vox", None, None), P(), P())
    out_specs = P("mode", None, "vox", None, None)
    return jax.shard_map(
        per_device, mesh=mesh, in_specs=in_specs, out_specs=out_specs, check_vma=False
    )
```

profile of v0, /device:TPU:1, one launch (start us, length us, event | category | flops | bytes accessed | tf_op | source)
XLA Modules:
  0.0 1051.0 jit_solution(3788761501652620217)
XLA Ops:
  6.5 1.2 copy_convert_fusion
  7.7 4.9 collective-permute-start.2
  12.7 5.8 collective-permute-start.3
  18.5 0.8 select_reduce_fusion
  19.3 1.9 collective-permute-start
  21.2 12.4 %collective-permute-start.1 = (f32[1,32,128]{2,1,0:T(8,128)S(1)}, f32[1,32,128]{2,1,0:T(8,128)S(1)}, u32[]{:S(2)}, u32[]{:S(2)}) collective-permute-start(f32[1,32,128]{2,1,0:T(8,128)S(1)} %bitcast.108), channel_id=1, source_target_pairs={{8,0},{16,8},{24,16},{32,24},{40,32},{48,40},{56,48},{64,56},{72,6... | collective-permute-start | bytes 49160 | tf_op jit(solution)/shard_map/ppermute | solution.py:17
  33.6 1.2 collective-permute-done.1
  35.1 2.2 select_maximum_fusion.4
  37.4 3.4 broadcast_multiply_fusion
  40.8 1.9 collective-permute-start.4
  42.7 12.6 %collective-permute-start.5 = (f32[16,3,1,32,128]{4,0,3,1,2:T(8,128)S(1)}, f32[16,3,1,32,128]{4,0,3,1,2:T(8,128)S(1)}, u32[]{:S(2)}, u32[]{:S(2)}) collective-permute-start(f32[16,3,1,32,128]{4,0,3,1,2:T(8,128)S(1)} %get-tuple-element.5), channel_id=1, source_target_pairs={{8,0},{16,8},{24,16},{32,24},{40,32},{48,40},{56,48},{64,56},{72,6... | collective-permute-start | bytes 2359304 | tf_op jit(solution)/shard_map/ppermute | solution.py:17
  55.4 1.9 collective-permute-done.5
  57.2 2.2 select_maximum_fusion.2
  59.4 3.4 convert_subtract_fusion
  62.9 1.9 collective-permute-start.6
  64.8 27.3 %collective-permute-start.7 = (f32[16,3,1,32,128]{4,0,3,1,2:T(8,128)S(1)}, f32[16,3,1,32,128]{4,0,3,1,2:T(8,128)S(1)}, u32[]{:S(2)}, u32[]{:S(2)}) collective-permute-start(f32[16,3,1,32,128]{4,0,3,1,2:T(8,128)S(1)} %convert_subtract_fusion), channel_id=1, source_target_pairs={{8,0},{16,8},{24,16},{32,24},{40,32},{48,40},{56,48},{64,56},{72,6... | collective-permute-start | bytes 2359304 | tf_op jit(solution)/shard_map/ppermute | solution.py:17
  92.1 1.9 collective-permute-done.7
  94.0 2.2 select_maximum_fusion
  96.2 4.0 fusion.66
  100.5 166.8 %all-gather.2.cloned.1.call-done = bf16[128,3,1,32,128]{4,0,3,1,2:T(8,128)(2,1)} async-done(((bf16[16,3,1,32,128]{4,0,3,1,2:T(8,128)(2,1)}), bf16[128,3,1,32,128]{4,0,3,1,2:T(8,128)(2,1)}) %all-gather.2.cloned.1.call-update) | async-done | bytes 3145744 | tf_op jit(solution)/shard_map/all_gather | solution.py:90
  267.2 4.4 fusion.6
  271.7 3.5 copy.17
  275.2 742.2 %all-reduce.6.cloned.1.call-done = f32[128,128]{0,1:T(8,128)} async-done(((f32[128,128]{0,1:T(8,128)}), f32[128,128]{0,1:T(8,128)}) %all-reduce.6.cloned.1.call-update) | async-done | bytes 65552 | tf_op jit(solution)/shard_map/psum | solution.py:92
  1017.4 0.9 copy.16
  1018.3 0.9 fusion.171
  1019.2 11.7 %cholesky.16 = f32[128,128]{1,0:T(8,128)S(1)} custom-call(f32[128,128]{1,0:T(8,128)S(1)} %fusion.171), custom_call_target="Cholesky" | custom-call | tf_op jit(solution)/shard_map/jit(cholesky)/cholesky | solution.py:43
  1031.0 0.6 compare_reduce_fusion
  1031.6 0.7 fusion.168
  1032.3 9.8 custom-call.6
  1042.1 0.3 fusion.169
  1042.4 0.9 fusion.5
  1043.3 0.8 copy.21
  (17 shorter events, 0.6 us)
Async XLA Ops:
  6.5 1035.5 %copy-start = (f32[128,128]{1,0:T(8,128)S(1)}, f32[128,128]{1,0:T(8,128)}, u32[]{:S(2)}) copy-start(f32[128,128]{1,0:T(8,128)} %param.7) | copy-start | bytes 196612
  6.5 30.8 %copy-start.1 = (bf16[16,3,1,32,128]{4,3,2,1,0:T(8,128)(2,1)S(1)}, bf16[16,3,1,32,128]{4,3,2,1,0:T(8,128)(2,1)}, u32[]{:S(2)}) copy-start(bf16[16,3,1,32,128]{4,3,2,1,0:T(8,128)(2,1)} %param.4) | copy-start | bytes 1179652
  6.5 260.7 %all-gather.2.cloned.1.call-start = ((), (), s32[]{:S(2)}) async-start(), calls=%async_computation | async-start | bytes 3538944 | tf_op jit(solution)/shard_map/all_gather | solution.py:90
  7.7 27.4 %collective-permute-start.2 = (f32[16,3,1,32,128]{4,0,3,1,2:T(8,128)S(1)}, f32[16,3,1,32,128]{4,0,3,1,2:T(8,128)S(1)}, u32[]{:S(2)}, u32[]{:S(2)}) collective-permute-start(f32[16,3,1,32,128]{4,0,3,1,2:T(8,128)S(1)} %copy_convert_fusion), channel_id=1, source_target_pairs={{0,8},{8,16},{16,24},{24,32},{32,40},{40,48},{48,56},{56,64},{64,7... | collective-permute-start | bytes 2359304 | tf_op jit(solution)/shard_map/ppermute | solution.py:16
  12.7 22.5 %collective-permute-start.3 = (f32[16,3,1,32,128]{4,0,3,1,2:T(8,128)S(1)}, f32[16,3,1,32,128]{4,0,3,1,2:T(8,128)S(1)}, u32[]{:S(2)}, u32[]{:S(2)}) collective-permute-start(f32[16,3,1,32,128]{4,0,3,1,2:T(8,128)S(1)} %copy_convert_fusion), channel_id=1, source_target_pairs={{8,0},{16,8},{24,16},{32,24},{40,32},{48,40},{56,48},{64,56},{72,6... | collective-permute-start | bytes 2359304 | tf_op jit(solution)/shard_map/ppermute | solution.py:17
  19.3 14.3 %collective-permute-start = (f32[1,32,128]{2,1,0:T(8,128)S(1)}, f32[1,32,128]{2,1,0:T(8,128)S(1)}, u32[]{:S(2)}, u32[]{:S(2)}) collective-permute-start(f32[1,32,128]{2,1,0:T(8,128)S(1)} %bitcast.107), channel_id=1, source_target_pairs={{0,8},{8,16},{16,24},{24,32},{32,40},{40,48},{48,56},{56,64},{64,7... | collective-permute-start | bytes 49160 | tf_op jit(solution)/shard_map/ppermute | solution.py:16
  21.2 13.6 %collective-permute-start.1 = (f32[1,32,128]{2,1,0:T(8,128)S(1)}, f32[1,32,128]{2,1,0:T(8,128)S(1)}, u32[]{:S(2)}, u32[]{:S(2)}) collective-permute-start(f32[1,32,128]{2,1,0:T(8,128)S(1)} %bitcast.108), channel_id=1, source_target_pairs={{8,0},{16,8},{24,16},{32,24},{40,32},{48,40},{56,48},{64,56},{72,6... | collective-permute-start | bytes 49160 | tf_op jit(solution)/shard_map/ppermute | solution.py:17
  40.8 14.5 %collective-permute-start.4 = (f32[16,3,1,32,128]{4,0,3,1,2:T(8,128)S(1)}, f32[16,3,1,32,128]{4,0,3,1,2:T(8,128)S(1)}, u32[]{:S(2)}, u32[]{:S(2)}) collective-permute-start(f32[16,3,1,32,128]{4,0,3,1,2:T(8,128)S(1)} %get-tuple-element.5), channel_id=1, source_target_pairs={{0,8},{8,16},{16,24},{24,32},{32,40},{40,48},{48,56},{56,64},{64,7... | collective-permute-start | bytes 2359304 | tf_op jit(solution)/shard_map/ppermute | solution.py:16
  42.7 14.5 %collective-permute-start.5 = (f32[16,3,1,32,128]{4,0,3,1,2:T(8,128)S(1)}, f32[16,3,1,32,128]{4,0,3,1,2:T(8,128)S(1)}, u32[]{:S(2)}, u32[]{:S(2)}) collective-permute-start(f32[16,3,1,32,128]{4,0,3,1,2:T(8,128)S(1)} %get-tuple-element.5), channel_id=1, source_target_pairs={{8,0},{16,8},{24,16},{32,24},{40,32},{48,40},{56,48},{64,56},{72,6... | collective-permute-start | bytes 2359304 | tf_op jit(solution)/shard_map/ppermute | solution.py:17
  62.9 29.2 %collective-permute-start.6 = (f32[16,3,1,32,128]{4,0,3,1,2:T(8,128)S(1)}, f32[16,3,1,32,128]{4,0,3,1,2:T(8,128)S(1)}, u32[]{:S(2)}, u32[]{:S(2)}) collective-permute-start(f32[16,3,1,32,128]{4,0,3,1,2:T(8,128)S(1)} %convert_subtract_fusion), channel_id=1, source_target_pairs={{0,8},{8,16},{16,24},{24,32},{32,40},{40,48},{48,56},{56,64},{64,7... | collective-permute-start | bytes 2359304 | tf_op jit(solution)/shard_map/ppermute | solution.py:16
  64.8 29.2 %collective-permute-start.7 = (f32[16,3,1,32,128]{4,0,3,1,2:T(8,128)S(1)}, f32[16,3,1,32,128]{4,0,3,1,2:T(8,128)S(1)}, u32[]{:S(2)}, u32[]{:S(2)}) collective-permute-start(f32[16,3,1,32,128]{4,0,3,1,2:T(8,128)S(1)} %convert_subtract_fusion), channel_id=1, source_target_pairs={{8,0},{16,8},{24,16},{32,24},{40,32},{48,40},{56,48},{64,56},{72,6... | collective-permute-start | bytes 2359304 | tf_op jit(solution)/shard_map/ppermute | solution.py:17
  100.2 917.2 %all-reduce.6.cloned.1.call-start = ((), (), s32[]{:S(2)}) async-start(), calls=%async_computation.1 | async-start | bytes 131072 | tf_op jit(solution)/shard_map/psum | solution.py:92
Sparse Core Ops, SparseCore 0:
  100.3 166.8 all-gather.1
  271.8 745.5 all-reduce.5
where the time goes:
time: 1050 us
  waiting for transfers between devices  914 us (87%)
  starting transfers between devices  68.9 us (7%)
  other arithmetic  43.5 us (4%)
  between operations  13.6 us (1%)
    psum x1, waiting for transfers between devices, per_device(): gram = lax.psum(gram_local(flat), 'vox')  742 us
    all_gather x1, waiting for transfers between devices, per_device(): every_mode = lax.all_gather(filtered, 'mode', axis=0, tiled=True)  167 us
    ppermute x4, starting transfers between devices, with_halo(): after = lax.ppermute(leading, axis, down)  58 us
  transfers between devices with their start and end apart: 10, of which 5 were waited for; matrix products, arithmetic and copies ran while one was open for 0% of the time, Pallas kernels for 0%

commit v1 on v0

v1 whole, which is shorter than its diff:
```python
import functools

import jax
import jax.numpy as jnp
from jax import lax
from jax.experimental import pallas as pl
from jax.experimental.pallas import tpu as pltpu
from jax.sharding import PartitionSpec as P

MESH = pl.DeviceIdType.MESH
F32 = jnp.float32
BF16 = jnp.bfloat16
E = 21.0
CENTRE = 35.0


class Sizes:
    def __init__(self, y, z_lo, z_hi, x, own=16, comps=3, nx=32, ny=128):
        self.y, self.z_lo, self.z_hi, self.x = y, z_lo, z_hi, x
        self.vox = y * z_lo * 2
        self.mode = z_hi * x
        self.own, self.comps, self.nx, self.ny = own, comps, nx, ny
        self.modes = self.mode * own
        self.rows = nx // x
        self.half = self.rows // z_hi
        self.group = x * y * 2
        self.zs = z_hi * z_lo
        self.piece = self.modes // self.group


class Place:
    def __init__(self, n):
        self.n = n
        self.v = lax.axis_index("vox")
        self.m = lax.axis_index("mode")
        self.y = lax.div(self.v, n.z_lo * 2)
        self.zl = lax.rem(lax.div(self.v, 2), n.z_lo)
        self.c = lax.rem(self.v, 2)
        self.zh = lax.div(self.m, n.x)
        self.x = lax.rem(self.m, n.x)
        self.g = (self.x * n.y + self.y) * 2 + self.c
        self.z = self.zh * n.z_lo + self.zl

    def in_group(self, g):
        n = self.n
        c, y, x = lax.rem(g, 2), lax.rem(lax.div(g, 2), n.y), lax.div(g, 2 * n.y)
        return {"vox": (y * n.z_lo + self.zl) * 2 + c, "mode": self.zh * n.x + x}

    def in_column(self, z):
        n = self.n
        zl, zh = lax.rem(z, n.z_lo), lax.div(z, n.z_lo)
        return {"vox": (self.y * n.z_lo + zl) * 2 + self.c, "mode": zh * n.x + self.x}


def remote(src, dst, send, recv, device):
    return pltpu.make_async_remote_copy(
        src_ref=src, dst_ref=dst, send_sem=send, recv_sem=recv,
        device_id=device, device_id_type=MESH,
    )


def meet(devices):
    barrier = pltpu.get_barrier_semaphore()
    for device in devices:
        pl.semaphore_signal(barrier, inc=1, device_id=device, device_id_type=MESH)
    pl.semaphore_wait(barrier, len(devices))


def filter_kernel(
    n, y0, cls, table, out_r,
    halo, shalo, sown, sm, sh, sp, dd, y1, y2, y1b, y2b, filt,
    hsend, hrecv, ssend, srecv, asend, arecv,
):
    me = Place(n)
    nxt = {"vox": lax.rem(me.v + 1, n.vox)}
    prv = {"vox": lax.rem(me.v + n.vox - 1, n.vox)}
    mates = [{"mode": lax.rem(me.m + d, n.mode)} for d in range(1, n.mode)]
    meet([nxt, prv] + mates)

    planes = cls[...]
    s = jnp.zeros((n.nx, n.ny), F32)
    for k in range(table.shape[0]):
        s = s + jnp.where(planes == k, table[k], 0.0)
    sown[...] = s
    scopies = [
        remote(sown, shalo.at[d], ssend.at[d], srecv.at[d], (nxt, prv)[d]) for d in range(2)
    ]
    for copy in scopies:
        copy.start()

    def hop(r, c, d):
        src = (y0, y1b, y2b)[r]
        return remote(
            src.at[c], halo.at[r, d, c], hsend.at[r, d, c], hrecv.at[r, d, c], (nxt, prv)[d]
        )

    for c in range(n.comps):
        for d in range(2):
            hop(0, c, d).start()

    lane = lax.broadcasted_iota(jnp.int32, (n.own, n.ny), 1)
    first, last = lane == 0, lane == n.ny - 1

    def along_y(u):
        before = jnp.where(first, 0.0, pltpu.roll(u, 1, 1))
        after = jnp.where(last, 0.0, pltpu.roll(u, n.ny - 1, 1))
        return (before + after) + (u + u)

    for copy in scopies:
        copy.wait()
    below, above = shalo[0], shalo[1]
    layers = below + above + (s + s)
    col = lax.broadcasted_iota(jnp.int32, (n.nx, n.ny), 1)
    row = lax.broadcasted_iota(jnp.int32, (n.nx, n.ny), 0)
    ty = (
        jnp.where(col == 0, 0.0, pltpu.roll(layers, 1, 1))
        + jnp.where(col == n.ny - 1, 0.0, pltpu.roll(layers, n.ny - 1, 1))
        + (layers + layers)
    )
    txy = (
        jnp.where(row == 0, 0.0, pltpu.roll(ty, 1, 0))
        + jnp.where(row == n.nx - 1, 0.0, pltpu.roll(ty, n.nx - 1, 0))
        + (ty + ty)
    )
    diag = (8.0 * s + 0.125 * txy - CENTRE) * (1.0 / E)
    part = 1.0 / (8.0 * E)
    for x in range(n.nx):
        wide = lambda a: jnp.broadcast_to(a[x : x + 1, :], (n.own, n.ny))
        sm[x] = wide(below * part)
        sh[x] = wide(s * (2.0 * part))
        sp[x] = wide(above * part)
        dd[x] = wide(diag)

    def stencil(r, c):
        def centre(x):
            if r == 0:
                return y0[c, x].astype(F32)
            return (y1, y2)[r - 1][c, x]

        def layer_sums(x):
            lo, mid, hi = halo[r, 0, c, x].astype(F32), centre(x), halo[r, 1, c, x].astype(F32)
            plain = (lo + hi) * 0.5 + mid
            weighted = sm[x] * lo + sh[x] * mid + sp[x] * hi
            return along_y(plain), along_y(weighted)

        def finish(x, a, b):
            value = dd[x] * centre(x) - (sh[x] * a + b)
            if r == 0:
                y1[c, x] = value
                y1b[c, x] = value.astype(BF16)
            elif r == 1:
                value = (value + value) - y0[c, x].astype(F32)
                y2[c, x] = value
                y2b[c, x] = value.astype(BF16)
            else:
                filt[c, x] = ((value + value) - y1[c, x]).astype(BF16)

        def body(x, carry):
            a0, a1, b0, b1 = carry
            a2, b2 = layer_sums(x + 1)
            finish(x, (a0 + a2) + (a1 + a1), (b0 + b2) + (b1 + b1))
            return a1, a2, b1, b2

        zero = jnp.zeros((n.own, n.ny), F32)
        a, b = layer_sums(0)
        a0, a1, b0, b1 = lax.fori_loop(0, n.nx - 1, body, (zero, a, zero, b))
        finish(n.nx - 1, a0 + (a1 + a1), b0 + (b1 + b1))

    def share(c, d, part):
        to = lax.rem(me.m + d, n.mode)
        to_x, to_zh = lax.rem(to, n.x), lax.div(to, n.x)
        at = lax.rem(to_zh + part, n.z_hi) * n.half
        src = filt.at[c, pl.ds(to_x * n.rows + at, n.half)]
        dst = out_r.at[c, pl.ds(at, n.half), pl.ds(pl.multiple_of(me.m * n.own, n.own), n.own)]
        return remote(src, dst, asend.at[part, c, d], arecv.at[part, c, d], {"mode": to})

    for r in range(3):
        for c in range(n.comps):
            for d in range(2):
                hop(r, c, d).wait_recv()
            stencil(r, c)
            if r < 2:
                for d in range(2):
                    hop(r + 1, c, d).start()
            else:
                for d in range(1, n.mode):
                    share(c, d, 0).start()
    for c in range(n.comps):
        for d in range(1, n.mode):
            share(c, d, 1).start()
        out_r[c, :, pl.ds(pl.multiple_of(me.m * n.own, n.own), n.own), :] = filt[
            c, pl.ds(me.x * n.rows, n.rows)
        ]
    for part in range(2):
        for c in range(n.comps):
            for d in range(1, n.mode):
                share(c, d, part).wait()
    for r in range(3):
        for c in range(n.comps):
            for d in range(2):
                hop(r, c, d).wait_send()


def run_filter(n, y0, cls, table):
    plane = (n.comps, n.nx, n.own, n.ny)
    vmem = pl.BlockSpec(memory_space=pltpu.VMEM)
    return pl.pallas_call(
        functools.partial(filter_kernel, n),
        out_shape=jax.ShapeDtypeStruct((n.comps, n.rows, n.modes, n.ny), BF16),
        in_specs=[vmem, vmem, pl.BlockSpec(memory_space=pltpu.SMEM)],
        out_specs=vmem,
        scratch_shapes=[
            pltpu.VMEM((3, 2) + plane, BF16),
            pltpu.VMEM((2, n.nx, n.ny), F32),
            pltpu.VMEM((n.nx, n.ny), F32),
        ]
        + [pltpu.VMEM((n.nx, n.own, n.ny), F32)] * 4
        + [pltpu.VMEM(plane, F32)] * 2
        + [pltpu.VMEM(plane, BF16)] * 3
        + [
            pltpu.SemaphoreType.DMA((3, 2, n.comps)),
            pltpu.SemaphoreType.DMA((3, 2, n.comps)),
            pltpu.SemaphoreType.DMA((2,)),
            pltpu.SemaphoreType.DMA((2,)),
            pltpu.SemaphoreType.DMA((2, n.comps, n.mode)),
            pltpu.SemaphoreType.DMA((2, n.comps, n.mode)),
        ],
        compiler_params=pltpu.CompilerParams(
            collective_id=1, has_side_effects=True, vmem_limit_bytes=40 << 20
        ),
        name="filter",
    )(y0, cls, table)


def gram_kernel(n, block, out, own, parts, column, total, send1, recv1, send2, recv2, send3, recv3):
    me = Place(n)
    group = [me.in_group(lax.rem(me.g + d, n.group)) for d in range(1, n.group)]
    stack = [me.in_column(lax.rem(me.z + d, n.zs)) for d in range(1, n.zs)]
    meet(group + stack)
    gram = jnp.zeros((n.modes, n.modes), F32)
    for c in range(n.comps):
        for k in range(n.half):
            a = block[c, me.zh * n.half + k]
            gram = gram + lax.dot_general(
                a, a, (((1,), (1,)), ((), ())), preferred_element_type=F32
            )
    for i in range(n.group):
        own[i] = gram[i * n.piece : (i + 1) * n.piece]

    def scatter(d):
        to = lax.rem(me.g + d, n.group)
        return remote(own.at[to], parts.at[d], send1.at[d], recv1.at[d], me.in_group(to))

    def around(d):
        to = lax.rem(me.z + d, n.zs)
        return remote(total, column.at[me.z], send2.at[d], recv2.at[d], me.in_column(to))

    def gather(d):
        to = lax.rem(me.g + d, n.group)
        return remote(total, out.at[me.g], send3.at[d], recv3.at[d], me.in_group(to))

    for d in range(1, n.group):
        scatter(d).start()
    mine = own[me.g]
    for d in range(1, n.group):
        scatter(d).wait()
        mine = mine + parts[d]
    total[...] = mine
    column[me.z] = mine
    for d in range(1, n.zs):
        around(d).start()
    for d in range(1, n.zs):
        around(d).wait()
    mine = column[0]
    for z in range(1, n.zs):
        mine = mine + column[z]
    total[...] = mine
    out[me.g] = mine
    for d in range(1, n.group):
        gather(d).start()
    for d in range(1, n.group):
        gather(d).wait()


def run_gram(n, block):
    vmem = pl.BlockSpec(memory_space=pltpu.VMEM)
    piece = (n.piece, n.modes)
    dma = pltpu.SemaphoreType.DMA
    return pl.pallas_call(
        functools.partial(gram_kernel, n),
        out_shape=jax.ShapeDtypeStruct((n.group,) + piece, F32),
        in_specs=[vmem],
        out_specs=vmem,
        scratch_shapes=[
            pltpu.VMEM((n.group,) + piece, F32),
            pltpu.VMEM((n.group,) + piece, F32),
            pltpu.VMEM((n.zs,) + piece, F32),
            pltpu.VMEM(piece, F32),
            dma((n.group,)), dma((n.group,)), dma((n.zs,)), dma((n.zs,)),
            dma((n.group,)), dma((n.group,)),
        ],
        compiler_params=pltpu.CompilerParams(
            collective_id=2, has_side_effects=True, vmem_limit_bytes=40 << 20
        ),
        name="gram",
    )(block)


def rotate_kernel(n, block, mix_t, out, held, send, recv):
    me = Place(n)
    meet([{"mode": me.zh * n.x + lax.rem(me.x + d, n.x)} for d in range(1, n.x)])
    mine = pl.ds(pl.multiple_of(me.x * n.own, n.own), n.own)

    def back(c, d):
        to = lax.rem(me.x + d, n.x)
        src = held.at[c, :, pl.ds(pl.multiple_of(to * n.own, n.own), n.own)]
        dst = out.at[c, pl.ds(me.x * n.rows, n.rows)]
        return remote(src, dst, send.at[c, d], recv.at[c, d], {"mode": me.zh * n.x + to})

    weights = mix_t[...]
    for c in range(n.comps):
        for k in range(n.rows):
            held[c, k] = jnp.dot(weights, block[c, k], preferred_element_type=F32).astype(BF16)
        for d in range(1, n.x):
            back(c, d).start()
    for c in range(n.comps):
        out[c, pl.ds(me.x * n.rows, n.rows)] = held[c, :, mine, :]
    for c in range(n.comps):
        for d in range(1, n.x):
            back(c, d).wait()


def run_rotate(n, block, mix_t):
    vmem = pl.BlockSpec(memory_space=pltpu.VMEM)
    return pl.pallas_call(
        functools.partial(rotate_kernel, n),
        out_shape=jax.ShapeDtypeStruct((n.comps, n.nx, n.own, n.ny), BF16),
        in_specs=[vmem, vmem],
        out_specs=vmem,
        scratch_shapes=[
            pltpu.VMEM((n.comps, n.rows, n.x * n.own, n.ny), BF16),
            pltpu.SemaphoreType.DMA((n.comps, n.x)),
            pltpu.SemaphoreType.DMA((n.comps, n.x)),
        ],
        compiler_params=pltpu.CompilerParams(
            collective_id=3, has_side_effects=True, vmem_limit_bytes=40 << 20
        ),
        name="rotate",
    )(block, mix_t)


def make_mix(gram, coefficients, total_rows):
    lower = jnp.linalg.cholesky(gram)
    solved = lax.linalg.triangular_solve(
        lower, coefficients, left_side=True, lower=True, transpose_a=True
    )
    return (solved * jnp.sqrt(jnp.float32(total_rows))).astype(BF16)


def per_device(n, modes_in, class_map, stiffness_table, coefficients):
    y0 = jnp.transpose(modes_in[:, :, 0], (1, 2, 0, 3))
    block = run_filter(n, y0, class_map[0], stiffness_table)
    gram = run_gram(n, block).reshape(n.modes, n.modes)
    mix = make_mix(gram, coefficients, n.comps * n.vox * n.nx * n.ny)
    width = n.x * n.own
    start = lax.div(lax.axis_index("mode"), n.x) * width
    mix_t = lax.dynamic_slice_in_dim(mix.T, start, width, 0)
    result = run_rotate(n, block, mix_t)
    return jnp.transpose(result, (2, 0, 1, 3))[:, :, None]


def build(mesh, n):
    spec = P("mode", None, "vox", None, None)
    return jax.shard_map(
        functools.partial(per_device, n), mesh=mesh,
        in_specs=(spec, P("vox", None, None), P(), P()), out_specs=spec, check_vma=False,
    )


def solution(mesh):
    return build(mesh, Sizes(y=4, z_lo=8, z_hi=2, x=4))
```

time: 1050 us -> 155 us (0.15)
  waiting for transfers between devices: 914 us -> 0 us
  Pallas kernels: 0 us -> 129 us
  starting transfers between devices: 68.9 us -> 0 us
  other arithmetic: 43.5 us -> 22.9 us
  between operations: 13.6 us -> 0.1 us
    psum x1 -> x0, waiting for transfers between devices: 742 us -> none  [per_device(): gram = lax.psum(gram_local(flat), 'vox')]
    all_gather x1 -> x0, waiting for transfers between devices: 167 us -> none  [per_device(): every_mode = lax.all_gather(filtered, 'mode', axis=0, tiled=True)]
    pallas_call x0 -> x3, Pallas kernels: none -> 129 us  [the longest x1 80.9 us: run_filter(): pl.pallas_call(functools.partial(filter_kernel, n), out_shape=jax.ShapeDt...]
    ppermute x8 -> x0, starting transfers between devices: 68.7 us -> none  [the longest x4 58 us: with_halo(): after = lax.ppermute(leading, axis, down)]
  transfers between devices with their start and end apart: 10 -> 0, of which waited for: 5 -> 0; matrix products, arithmetic and copies ran while one was open for 0% -> 0% of each run, Pallas kernels for 0% -> 0%
where the time goes in v1:
time: 155 us
  Pallas kernels  129 us (83%)
  other arithmetic  22.9 us (15%)
  local copies, waits for them, and re-layouts  2.78 us (2%)
    pallas_call x1, Pallas kernels, run_filter(): pl.pallas_call(functools.partial(filter_kernel, n), out_shape=jax.ShapeDt...  80.9 us
    pallas_call x1, Pallas kernels, run_gram(): pl.pallas_call(functools.partial(gram_kernel, n), out_shape=jax.ShapeDtyp...  39.1 us
    another operation x3, other arithmetic, make_mix(): lower = jnp.linalg.cholesky(gram)  12.4 us
    another operation x2, other arithmetic, make_mix(): lax.linalg.triangular_solve(lower, coefficients, left_side=True, lower=Tr...  10.5 us
    pallas_call x1, Pallas kernels, run_rotate(): pl.pallas_call(functools.partial(rotate_kernel, n), out_shape=jax.ShapeDt...  8.73 us

profile of v1, /device:TPU:1, one launch (start us, length us, event | category | flops | bytes accessed | tf_op | source)
XLA Modules:
  0.0 154.7 jit_solution(17308509972776014427)
XLA Ops:
  0.0 0.0 copy-start
  0.0 0.0 copy-start.1
  0.0 1.2 copy.13
  1.2 0.0 copy-start.2
  1.2 0.0 copy-done.1
  1.2 0.6 copy-done.2
  1.9 80.9 %filter.1.block = bf16[3,8,128,128]{3,2,1,0:T(8,128)(2,1)S(1)} custom-call(bf16[3,32,16,128]{3,2,1,0:T(8,128)(2,1)S(1)} %bitcast.23, s32[32,128]{1,0:T(8,128)S(1)} %bitcast.26, f32[8]{0:T(128)S(1)} %copy-done.2), custom_call_target="tpu_custom_call" | custom-call | tf_op jit(solution)/shard_map/filter/pallas_call | solution.py:207
  82.8 39.1 %gram.1 = f32[32,4,128]{2,1,0:T(4,128)S(1)} custom-call(bf16[3,8,128,128]{3,2,1,0:T(8,128)(2,1)S(1)} %filter.1.block), custom_call_target="tpu_custom_call" | custom-call | tf_op jit(solution)/shard_map/gram/pallas_call | solution.py:289
  121.8 0.1 copy.10
  122.0 11.7 %cholesky.16 = f32[128,128]{1,0:T(8,128)S(1)} custom-call(f32[128,128]{1,0:T(8,128)S(1)} %fusion.3), custom_call_target="Cholesky" | custom-call | tf_op jit(solution)/shard_map/jit(cholesky)/cholesky | solution.py:353
  133.7 0.6 compare_reduce_fusion
  134.3 0.7 fusion
  135.0 9.8 %custom-call.6 = f32[1,128,128]{1,2,0:T(8,128)S(1)} custom-call(f32[1,128,128]{2,1,0:T(8,128)S(1)} %fusion), custom_call_target="InvertDiagBlocksLowerTriangular" | custom-call | tf_op jit(solution)/shard_map/triangular_solve | solution.py:354
  144.8 0.0 copy-done
  144.8 0.3 fusion.1
  145.1 8.7 %rotate.1 = bf16[3,32,16,128]{3,2,1,0:T(8,128)(2,1)S(1)} custom-call(bf16[3,8,128,128]{3,2,1,0:T(8,128)(2,1)S(1)} %filter.1.block, bf16[64,128]{1,0:T(8,128)(2,1)S(1)} %fusion.5.mix_t), custom_call_target="tpu_custom_call" | custom-call | tf_op jit(solution)/shard_map/rotate/pallas_call | solution.py:335
  153.9 0.8 copy.11
  (3 shorter events, 0.1 us)
Async XLA Ops:
  0.0 144.8 %copy-start = (f32[128,128]{1,0:T(8,128)S(1)}, f32[128,128]{1,0:T(8,128)}, u32[]{:S(2)}) copy-start(f32[128,128]{1,0:T(8,128)} %param.7) | copy-start | bytes 196612
  0.0 1.2 copy-start.1
  1.2 0.7 copy-start.2

commit v2 on v1

v2 whole, which is shorter than its diff:
```python
import functools
import math

import jax
import jax.numpy as jnp
from jax import lax
from jax.experimental import pallas as pl
from jax.experimental.pallas import tpu as pltpu
from jax.sharding import PartitionSpec as P

MESH = pl.DeviceIdType.MESH
F32 = jnp.float32
BF16 = jnp.bfloat16
E = 21.0
CENTRE = 35.0


class Sizes:
    def __init__(self, y, z_lo, z_hi, x, own=16, comps=3, nx=32, ny=128):
        self.y, self.z_lo, self.z_hi, self.x = y, z_lo, z_hi, x
        self.vox = y * z_lo * 2
        self.mode = z_hi * x
        self.own, self.comps, self.nx, self.ny = own, comps, nx, ny
        self.modes = self.mode * own
        self.rows = nx // x
        self.half = self.rows // z_hi
        self.group = x * y * 2
        self.zs = z_hi * z_lo
        self.piece = self.modes // self.group


class Place:
    def __init__(self, n):
        self.n = n
        self.v = lax.axis_index("vox")
        self.m = lax.axis_index("mode")
        self.y = lax.div(self.v, n.z_lo * 2)
        self.zl = lax.rem(lax.div(self.v, 2), n.z_lo)
        self.c = lax.rem(self.v, 2)
        self.zh = lax.div(self.m, n.x)
        self.x = lax.rem(self.m, n.x)
        self.g = (self.x * n.y + self.y) * 2 + self.c
        self.z = self.zh * n.z_lo + self.zl

    def in_group(self, dx, dy, dc):
        n = self.n
        x, y, c = lax.rem(self.x + dx, n.x), lax.rem(self.y + dy, n.y), lax.rem(self.c + dc, 2)
        device = {"vox": (y * n.z_lo + self.zl) * 2 + c, "mode": self.zh * n.x + x}
        return device, (x * n.y + y) * 2 + c

    def in_column(self, z):
        n = self.n
        zl, zh = lax.rem(z, n.z_lo), lax.div(z, n.z_lo)
        return {"vox": (self.y * n.z_lo + zl) * 2 + self.c, "mode": zh * n.x + self.x}


def remote(src, dst, send, recv, device):
    return pltpu.make_async_remote_copy(
        src_ref=src, dst_ref=dst, send_sem=send, recv_sem=recv,
        device_id=device, device_id_type=MESH,
    )


def sum_rows(a, before, after):
    return (before + after) + (a + a)


def whiten(gram, size, scale):
    row = lax.broadcasted_iota(jnp.int32, (size, size), 0)
    rest = gram
    inverse = jnp.where(row == lax.broadcasted_iota(jnp.int32, (size, size), 1), 1.0, 0.0)
    sub = row[:8]
    done = []
    for k in range(size // 8):
        left = size - 8 * k
        wide = lambda a, i: jnp.broadcast_to(a[i : i + 1], (left, size))
        cols = [
            jnp.broadcast_to(rest[:, 8 * k + j : 8 * k + j + 1], (left, size)) for j in range(8)
        ]
        root = jnp.zeros((8, size), F32)
        for i in range(8):
            pivot = cols[i][i : i + 1]
            inv = 1.0 / pivot
            factor = jnp.where(row[:left] > i, cols[i], 0.0) * jnp.broadcast_to(inv, (left, size))
            for j in range(i + 1, 8):
                cols[j] = cols[j] - factor * wide(cols[j], i)
            rest = rest - factor * wide(rest, i)
            inverse = inverse - factor * wide(inverse, i)
            root = jnp.where(sub == i, jnp.broadcast_to(lax.rsqrt(pivot) * scale, (8, size)), root)
        done.append(inverse[:8] * root)
        rest, inverse = rest[8:], inverse[8:]
    return done


def kernel(
    n, y0, cls, table, coef_t, out,
    halo, shalo, sown, sm, sh, sp, dd, y1, y2, y1b, y2b, filt, block,
    own, parts, column, total, pieces, gram, white, held,
    hsend, hrecv, ssend, srecv, asend, arecv,
    send1, recv1, send2, recv2, send3, recv3, send4, recv4,
):
    me = Place(n)
    nxt = {"vox": lax.rem(me.v + 1, n.vox)}
    prv = {"vox": lax.rem(me.v + n.vox - 1, n.vox)}
    far = lambda d, size: min(d, size - d)
    steps = [(dx, dy, dc) for dx in range(n.x) for dy in range(n.y) for dc in range(2)]
    steps = sorted(steps[1:], key=lambda s: (-far(s[0], n.x) - far(s[1], n.y), s))
    climbs = sorted(range(1, n.zs), key=lambda d: (-far(d, n.zs), d))

    barrier = pltpu.get_barrier_semaphore()
    friends = [nxt, prv]
    friends += [me.in_group(*step)[0] for step in steps]
    friends += [me.in_column(lax.rem(me.z + d, n.zs)) for d in climbs]
    for dz in range(1, n.z_hi):
        for dx in range(1, n.x):
            friends.append({
                "mode": lax.rem(me.zh + dz, n.z_hi) * n.x + lax.rem(me.x + dx, n.x)
            })
    for device in friends:
        pl.semaphore_signal(barrier, inc=1, device_id=device, device_id_type=MESH)

    planes = cls[...]
    s = jnp.zeros((n.nx, n.ny), F32)
    for k in range(table.shape[0]):
        s = s + jnp.where(planes == k, table[k], 0.0)
    sown[...] = s
    pl.semaphore_wait(barrier, len(friends))

    scopies = [
        remote(sown, shalo.at[d], ssend.at[d], srecv.at[d], (nxt, prv)[d]) for d in range(2)
    ]
    for copy in scopies:
        copy.start()

    def hop(r, c, d):
        src = (y0, y1b, y2b)[r]
        return remote(
            src.at[c], halo.at[r, d, c], hsend.at[r, d, c], hrecv.at[r, d, c], (nxt, prv)[d]
        )

    for c in range(n.comps):
        for d in range(2):
            hop(0, c, d).start()

    for copy in scopies:
        copy.wait()
    below, above = shalo[0], shalo[1]
    col = lax.broadcasted_iota(jnp.int32, (n.nx, n.ny), 1)
    row = lax.broadcasted_iota(jnp.int32, (n.nx, n.ny), 0)
    layers = sum_rows(s, below, above)
    ty = sum_rows(
        layers,
        jnp.where(col == 0, 0.0, pltpu.roll(layers, 1, 1)),
        jnp.where(col == n.ny - 1, 0.0, pltpu.roll(layers, n.ny - 1, 1)),
    )
    txy = sum_rows(
        ty,
        jnp.where(row == 0, 0.0, pltpu.roll(ty, 1, 0)),
        jnp.where(row == n.nx - 1, 0.0, pltpu.roll(ty, n.nx - 1, 0)),
    )
    diag = (8.0 * s + 0.125 * txy - CENTRE) * (1.0 / E)
    part = 1.0 / (8.0 * E)
    for held_in, values in ((sm, below * part), (sh, s * (2.0 * part)), (sp, above * part), (dd, diag)):
        for x in range(n.nx):
            held_in[x] = jnp.broadcast_to(values[x : x + 1, :], (n.own, n.ny))

    strip = 4
    lane = lax.broadcasted_iota(jnp.int32, (n.own, n.ny), 1)
    first, last = lane == 0, lane == n.ny - 1

    def along_y(u):
        rows = []
        for i in range(u.shape[0]):
            v = u[i]
            before = jnp.where(first, 0.0, pltpu.roll(v, 1, 1))
            after = jnp.where(last, 0.0, pltpu.roll(v, n.ny - 1, 1))
            rows.append(sum_rows(v, before, after))
        return jnp.stack(rows)

    def stencil(r, c):
        def centre(at):
            if r == 0:
                return y0[c, at].astype(F32)
            return (y1, y2)[r - 1][c, at]

        def layer_sums(lo_row, hi_row):
            at = slice(lo_row, hi_row)
            lo, mid, hi = halo[r, 0, c, at].astype(F32), centre(at), halo[r, 1, c, at].astype(F32)
            plain = (lo + hi) * 0.5 + mid
            weighted = sm[at] * lo + sh[at] * mid + sp[at] * hi
            return along_y(plain), along_y(weighted)

        zero = jnp.zeros((1, n.own, n.ny), F32)
        a, b = layer_sums(0, 1)
        a, b = jnp.concatenate([zero, a]), jnp.concatenate([zero, b])
        for x in range(0, n.nx, strip):
            at = slice(x, x + strip)
            more = list(layer_sums(x + 1, min(x + strip + 1, n.nx)))
            if x + strip == n.nx:
                more = [jnp.concatenate([u, zero]) for u in more]
            a, b = jnp.concatenate([a, more[0]]), jnp.concatenate([b, more[1]])
            fold = lambda u: sum_rows(u[1 : strip + 1], u[:strip], u[2:])
            value = dd[at] * centre(at) - (sh[at] * fold(a) + fold(b))
            a, b = a[strip:], b[strip:]
            if r == 0:
                y1[c, at] = value
                y1b[c, at] = value.astype(BF16)
            elif r == 1:
                value = (value + value) - y0[c, at].astype(F32)
                y2[c, at] = value
                y2b[c, at] = value.astype(BF16)
            else:
                filt[c, at] = ((value + value) - y1[c, at]).astype(BF16)

    mine = pl.ds(pl.multiple_of(me.m * n.own, n.own), n.own)

    def share(c, d, part):
        to = lax.rem(me.m + d, n.mode)
        to_x, to_zh = lax.rem(to, n.x), lax.div(to, n.x)
        at = lax.rem(to_zh + part, n.z_hi) * n.half
        src = filt.at[c, pl.ds(to_x * n.rows + at, n.half)]
        dst = block.at[c, pl.ds(at, n.half), mine]
        return remote(src, dst, asend.at[part, c, d], arecv.at[part, c, d], {"mode": to})

    shares = range(1, n.mode)
    for r in range(3):
        for c in range(n.comps):
            for d in range(2):
                hop(r, c, d).wait_recv()
            stencil(r, c)
            if r < 2:
                for d in range(2):
                    hop(r + 1, c, d).start()
            else:
                for d in shares:
                    share(c, d, 0).start()
                block[c, :, mine, :] = filt[c, pl.ds(me.x * n.rows, n.rows)]
    for d in shares:
        share(0, d, 1).start()

    product = jnp.zeros((n.modes, n.modes), F32)
    for c in range(n.comps):
        for d in shares:
            share(c, d, 0).wait_recv()
        for k in range(n.half):
            a = block[c, me.zh * n.half + k]
            product = product + lax.dot_general(
                a, a, (((1,), (1,)), ((), ())), preferred_element_type=F32
            )
    for i in range(n.group):
        own[i] = product[i * n.piece : (i + 1) * n.piece]

    def scatter(i):
        device, to = me.in_group(*steps[i])
        return remote(own.at[to], parts.at[i], send1.at[i], recv1.at[i], device)

    def around(d):
        to = me.in_column(lax.rem(me.z + d, n.zs))
        return remote(total, column.at[me.z], send2.at[d], recv2.at[d], to)

    def gather(i):
        device = me.in_group(*steps[i])[0]
        return remote(column.at[n.zs], pieces.at[me.g], send3.at[i], recv3.at[i], device)

    for i in range(len(steps)):
        scatter(i).start()
    piece = own[me.g]
    for i in range(len(steps)):
        scatter(i).wait_recv()
        piece = piece + parts[i]
    total[...] = piece
    column[me.z] = piece
    for d in climbs:
        around(d).start()
    for d in climbs:
        around(d).wait_recv()
    piece = column[0]
    for z in range(1, n.zs):
        piece = piece + column[z]
    column[n.zs] = piece
    pieces[me.g] = piece
    for i in range(len(steps)):
        gather(i).start()
    for c in range(1, n.comps):
        for d in shares:
            share(c, d, 1).start()
    for i in range(len(steps)):
        gather(i).wait_recv()
    for i in range(n.group):
        gram[i * n.piece : (i + 1) * n.piece, :] = pieces[i]

    scale = math.sqrt(n.comps * n.vox * n.nx * n.ny)
    for k, rows in enumerate(whiten(gram[...], n.modes, scale)):
        white[8 * k : 8 * k + 8, :] = rows
    mix_t = jnp.dot(
        coef_t[...], white[...], precision=lax.Precision.HIGHEST, preferred_element_type=F32
    ).astype(BF16)

    def back(c, d):
        to = lax.rem(me.x + d, n.x)
        src = held.at[c, :, pl.ds(pl.multiple_of(to * n.own, n.own), n.own)]
        dst = out.at[c, pl.ds(me.x * n.rows, n.rows)]
        return remote(src, dst, send4.at[c, d], recv4.at[c, d], {"mode": me.zh * n.x + to})

    kept = pl.ds(pl.multiple_of(me.x * n.own, n.own), n.own)
    for c in range(n.comps):
        for d in shares:
            share(c, d, 1).wait_recv()
        for k in range(n.rows):
            held[c, k] = jnp.dot(mix_t, block[c, k], preferred_element_type=F32).astype(BF16)
        for d in range(1, n.x):
            back(c, d).start()
        out[c, pl.ds(me.x * n.rows, n.rows)] = held[c, :, kept, :]

    for c in range(n.comps):
        for r in range(3):
            for d in range(2):
                hop(r, c, d).wait_send()
        for d in shares:
            share(c, d, 0).wait_send()
            share(c, d, 1).wait_send()
    for i in range(len(steps)):
        scatter(i).wait_send()
        gather(i).wait_send()
    for d in climbs:
        around(d).wait_send()
    for c in range(n.comps):
        for d in range(1, n.x):
            back(c, d).wait()


def run(n, y0, cls, table, coef_t):
    plane = (n.comps, n.nx, n.own, n.ny)
    piece = (n.piece, n.modes)
    square = (n.modes, n.modes)
    vmem = pl.BlockSpec(memory_space=pltpu.VMEM)
    dma = lambda *shape: [pltpu.SemaphoreType.DMA(shape)] * 2
    return pl.pallas_call(
        functools.partial(kernel, n),
        out_shape=jax.ShapeDtypeStruct(plane, BF16),
        in_specs=[vmem, vmem, pl.BlockSpec(memory_space=pltpu.SMEM), vmem],
        out_specs=vmem,
        scratch_shapes=[
            pltpu.VMEM((3, 2) + plane, BF16),
            pltpu.VMEM((2, n.nx, n.ny), F32),
            pltpu.VMEM((n.nx, n.ny), F32),
        ]
        + [pltpu.VMEM((n.nx, n.own, n.ny), F32)] * 4
        + [pltpu.VMEM(plane, F32)] * 2
        + [pltpu.VMEM(plane, BF16)] * 3
        + [
            pltpu.VMEM((n.comps, n.rows, n.modes, n.ny), BF16),
            pltpu.VMEM((n.group,) + piece, F32),
            pltpu.VMEM((n.group,) + piece, F32),
            pltpu.VMEM((n.zs + 1,) + piece, F32),
            pltpu.VMEM(piece, F32),
            pltpu.VMEM((n.group,) + piece, F32),
            pltpu.VMEM(square, F32),
            pltpu.VMEM(square, F32),
            pltpu.VMEM((n.comps, n.rows, n.x * n.own, n.ny), BF16),
        ]
        + dma(3, 2, n.comps) + dma(2) + dma(2, n.comps, n.mode)
        + dma(n.group) + dma(n.zs) + dma(n.group) + dma(n.comps, n.x),
        compiler_params=pltpu.CompilerParams(
            collective_id=1, has_side_effects=True, vmem_limit_bytes=48 << 20
        ),
        name="ritz",
    )(y0, cls, table, coef_t)


def per_device(n, modes_in, class_map, stiffness_table, coefficients):
    y0 = jnp.transpose(modes_in[:, :, 0], (1, 2, 0, 3))
    width = n.x * n.own
    start = lax.div(lax.axis_index("mode"), n.x) * width
    coef_t = lax.dynamic_slice_in_dim(coefficients.T, start, width, 0)
    result = run(n, y0, class_map[0], stiffness_table, coef_t)
    return jnp.transpose(result, (2, 0, 1, 3))[:, :, None]


def build(mesh, n):
    spec = P("mode", None, "vox", None, None)
    return jax.shard_map(
        functools.partial(per_device, n), mesh=mesh,
        in_specs=(spec, P("vox", None, None), P(), P()), out_specs=spec, check_vma=False,
    )


def solution(mesh):
    return build(mesh, Sizes(y=4, z_lo=8, z_hi=2, x=4))
```

time: 155 us -> 110 us (0.71)
  Pallas kernels: 129 us -> 106 us
  other arithmetic: 22.9 us -> 0 us
    another operation x5 -> x0, other arithmetic: 22.9 us -> none  [the longest x3 12.4 us: make_mix(): lower = jnp.linalg.cholesky(gram)]
    pallas_call x3 -> x1, Pallas kernels: 129 us -> 106 us  [run(): pl.pallas_call(functools.partial(kernel, n), out_shape=jax.ShapeDtypeStru...]
where the time goes in v2:
time: 110 us
  Pallas kernels  106 us (96%)
  local copies, waits for them, and re-layouts  3.66 us (3%)
    pallas_call x1, Pallas kernels, run(): pl.pallas_call(functools.partial(kernel, n), out_shape=jax.ShapeDtypeStru...  106 us
    unnamed x8, local copies, waits for them, and re-layouts  2.74 us

profile of v2, /device:TPU:1, one launch (start us, length us, event | category | flops | bytes accessed | tf_op | source)
XLA Modules:
  0.0 109.7 jit_solution(795988110147710892)
XLA Ops:
  0.0 0.0 copy-start
  0.0 0.8 copy-done
  0.8 0.1 constant_dynamic-slice_fusion
  0.9 0.1 copy.8
  1.0 0.0 copy-start.1
  1.0 1.2 %copy.10 = bf16[16,3,1,32,128]{4,0,3,1,2:T(8,128)(2,1)S(1)} copy(bf16[16,3,1,32,128]{4,3,2,1,0:T(8,128)(2,1)} %param.4) | data formatting | bytes 786432 | tf_op args[0]
  2.2 0.0 copy-start.2
  2.2 0.0 copy-done.1
  2.2 0.6 copy-done.2
  2.8 106.0 %ritz.1 = bf16[3,32,16,128]{3,2,1,0:T(8,128)(2,1)S(1)} custom-call(bf16[3,32,16,128]{3,2,1,0:T(8,128)(2,1)S(1)} %bitcast.11, s32[32,128]{1,0:T(8,128)S(1)} %bitcast.13, f32[8]{0:T(128)S(1)} %copy-done.2, f32[64,128]{1,0:T(8,128)S(1)} %bitcast.12), custom_call_target="tpu_custom_call" | custom-call | tf_op jit(solution)/shard_map/ritz/pallas_call | solution.py:338
  108.9 0.8 copy.7
Async XLA Ops:
  0.0 0.8 copy-start
  1.0 1.2 %copy-start.1 = (s32[1,32,128]{2,1,0:T(8,128)S(1)}, s32[1,32,128]{2,1,0:T(8,128)}, u32[]{:S(2)}) copy-start(s32[1,32,128]{2,1,0:T(8,128)} %param.5) | copy-start | bytes 49156
  2.2 0.7 copy-start.2

commit v3 on v2

--- a/solution.py
+++ b/solution.py
@@ -93,8 +93,8 @@
 
 
 def kernel(
-    n, y0, cls, table, coef_t, out,
-    halo, shalo, sown, sm, sh, sp, dd, y1, y2, y1b, y2b, filt, block,
+    n, modes_hbm, cls_hbm, table_hbm, coef_hbm, out,
+    raw, cls, table, coef, loaded, mixed, y0, halo, shalo, sown, sm, sh, sp, dd, y1, y2, y1b, y2b, filt, block,
     own, parts, column, total, pieces, gram, white, held,
     hsend, hrecv, ssend, srecv, asend, arecv,
     send1, recv1, send2, recv2, send3, recv3, send4, recv4,
@@ -107,6 +107,18 @@
     steps = sorted(steps[1:], key=lambda s: (-far(s[0], n.x) - far(s[1], n.y), s))
     climbs = sorted(range(1, n.zs), key=lambda d: (-far(d, n.zs), d))
 
+    loads = [
+        pltpu.make_async_copy(cls_hbm, cls, loaded.at[0]),
+        pltpu.make_async_copy(table_hbm, table, loaded.at[1]),
+        pltpu.make_async_copy(coef_hbm, coef, loaded.at[2]),
+    ]
+    loads += [
+        pltpu.make_async_copy(modes_hbm.at[:, c], raw.at[:, c], loaded.at[3 + c])
+        for c in range(n.comps)
+    ]
+    for load in loads:
+        load.start()
+
     barrier = pltpu.get_barrier_semaphore()
     friends = [nxt, prv]
     friends += [me.in_group(*step)[0] for step in steps]
@@ -119,11 +131,30 @@
     for device in friends:
         pl.semaphore_signal(barrier, inc=1, device_id=device, device_id_type=MESH)
 
+    size = n.own * n.own
+    at_row = lax.broadcasted_iota(jnp.int32, (size, size), 0)
+    at_col = lax.broadcasted_iota(jnp.int32, (size, size), 1)
+    swap = jnp.where(
+        at_col == lax.rem(at_row, n.own) * n.own + lax.div(at_row, n.own), 1.0, 0.0
+    ).astype(BF16)
+
+    def turn(c):
+        for x in range(0, n.nx, n.own):
+            tile = raw[:, c, x : x + n.own, :].reshape(size, n.ny)
+            turned = jnp.dot(swap, tile, preferred_element_type=F32).astype(BF16)
+            y0[c, x : x + n.own] = turned.reshape(n.own, n.own, n.ny)
+
+    for load in loads[:2]:
+        load.wait()
     planes = cls[...]
     s = jnp.zeros((n.nx, n.ny), F32)
     for k in range(table.shape[0]):
         s = s + jnp.where(planes == k, table[k], 0.0)
     sown[...] = s
+    for c in range(n.comps):
+        loads[3 + c].wait()
+        turn(c)
+    loads[2].wait()
     pl.semaphore_wait(barrier, len(friends))
 
     scopies = [
@@ -132,15 +163,23 @@
     for copy in scopies:
         copy.start()
 
-    def hop(r, c, d):
+    strip = 4
+    cuts = [n.nx // 2 + strip, n.nx // 2, n.nx // 2 - strip, n.nx // 2 - 2 * strip]
+    parts_of = lambda r: (slice(0, cuts[r]), slice(cuts[r], n.nx))
+
+    def hop(r, c, d, p):
         src = (y0, y1b, y2b)[r]
+        rows = parts_of(r)[p]
+        at = pl.ds(rows.start, rows.stop - rows.start)
         return remote(
-            src.at[c], halo.at[r, d, c], hsend.at[r, d, c], hrecv.at[r, d, c], (nxt, prv)[d]
+            src.at[c, at], halo.at[r, d, c, at],
+            hsend.at[r, d, c, p], hrecv.at[r, d, c, p], (nxt, prv)[d],
         )
 
     for c in range(n.comps):
-        for d in range(2):
-            hop(0, c, d).start()
+        for p in range(2):
+            for d in range(2):
+                hop(0, c, d, p).start()
 
     for copy in scopies:
         copy.wait()
@@ -164,7 +203,6 @@
         for x in range(n.nx):
             held_in[x] = jnp.broadcast_to(values[x : x + 1, :], (n.own, n.ny))
 
-    strip = 4
     lane = lax.broadcasted_iota(jnp.int32, (n.own, n.ny), 1)
     first, last = lane == 0, lane == n.ny - 1
 
@@ -177,7 +215,7 @@
             rows.append(sum_rows(v, before, after))
         return jnp.stack(rows)
 
-    def stencil(r, c):
+    def stencil(r, c, arrive, leave):
         def centre(at):
             if r == 0:
                 return y0[c, at].astype(F32)
@@ -191,10 +229,14 @@
             return along_y(plain), along_y(weighted)
 
         zero = jnp.zeros((1, n.own, n.ny), F32)
+        arrive(0)
         a, b = layer_sums(0, 1)
         a, b = jnp.concatenate([zero, a]), jnp.concatenate([zero, b])
         for x in range(0, n.nx, strip):
             at = slice(x, x + strip)
+            if x + strip == cuts[r]:
+                leave(0)
+                arrive(1)
             more = list(layer_sums(x + 1, min(x + strip + 1, n.nx)))
             if x + strip == n.nx:
                 more = [jnp.concatenate([u, zero]) for u in more]
@@ -211,6 +253,7 @@
                 y2b[c, at] = value.astype(BF16)
             else:
                 filt[c, at] = ((value + value) - y1[c, at]).astype(BF16)
+        leave(1)
 
     mine = pl.ds(pl.multiple_of(me.m * n.own, n.own), n.own)
 
@@ -225,13 +268,17 @@
     shares = range(1, n.mode)
     for r in range(3):
         for c in range(n.comps):
-            for d in range(2):
-                hop(r, c, d).wait_recv()
-            stencil(r, c)
-            if r < 2:
+            def arrive(p):
                 for d in range(2):
-                    hop(r + 1, c, d).start()
-            else:
+                    hop(r, c, d, p).wait_recv()
+
+            def leave(p):
+                if r < 2:
+                    for d in range(2):
+                        hop(r + 1, c, d, p).start()
+
+            stencil(r, c, arrive, leave)
+            if r == 2:
                 for d in shares:
                     share(c, d, 0).start()
                 block[c, :, mine, :] = filt[c, pl.ds(me.x * n.rows, n.rows)]
@@ -292,9 +339,12 @@
     scale = math.sqrt(n.comps * n.vox * n.nx * n.ny)
     for k, rows in enumerate(whiten(gram[...], n.modes, scale)):
         white[8 * k : 8 * k + 8, :] = rows
-    mix_t = jnp.dot(
-        coef_t[...], white[...], precision=lax.Precision.HIGHEST, preferred_element_type=F32
-    ).astype(BF16)
+    mixed[...] = lax.dot_general(
+        coef[...], white[...], (((0,), (0,)), ((), ())),
+        precision=lax.Precision.HIGHEST, preferred_element_type=F32,
+    )
+    width = n.x * n.own
+    mix_t = mixed[pl.ds(pl.multiple_of(me.zh * width, width), width), :].astype(BF16)
 
     def back(c, d):
         to = lax.rem(me.x + d, n.x)
@@ -315,7 +365,8 @@
     for c in range(n.comps):
         for r in range(3):
             for d in range(2):
-                hop(r, c, d).wait_send()
+                for p in range(2):
+                    hop(r, c, d, p).wait_send()
         for d in shares:
             share(c, d, 0).wait_send()
             share(c, d, 1).wait_send()
@@ -329,7 +380,7 @@
             back(c, d).wait()
 
 
-def run(n, y0, cls, table, coef_t):
+def run(n, modes_in, class_map, table, coefficients):
     plane = (n.comps, n.nx, n.own, n.ny)
     piece = (n.piece, n.modes)
     square = (n.modes, n.modes)
@@ -338,9 +389,16 @@
     return pl.pallas_call(
         functools.partial(kernel, n),
         out_shape=jax.ShapeDtypeStruct(plane, BF16),
-        in_specs=[vmem, vmem, pl.BlockSpec(memory_space=pltpu.SMEM), vmem],
+        in_specs=[pl.BlockSpec(memory_space=pltpu.HBM)] * 4,
         out_specs=vmem,
         scratch_shapes=[
+            pltpu.VMEM((n.own, n.comps, n.nx, n.ny), BF16),
+            pltpu.VMEM((n.nx, n.ny), jnp.int32),
+            pltpu.SMEM(table.shape, F32),
+            pltpu.VMEM(square, F32),
+            pltpu.SemaphoreType.DMA((3 + n.comps,)),
+            pltpu.VMEM(square, F32),
+            pltpu.VMEM(plane, BF16),
             pltpu.VMEM((3, 2) + plane, BF16),
             pltpu.VMEM((2, n.nx, n.ny), F32),
             pltpu.VMEM((n.nx, n.ny), F32),
@@ -359,21 +417,17 @@
             pltpu.VMEM(square, F32),
             pltpu.VMEM((n.comps, n.rows, n.x * n.own, n.ny), BF16),
         ]
-        + dma(3, 2, n.comps) + dma(2) + dma(2, n.comps, n.mode)
+        + dma(3, 2, n.comps, 2) + dma(2) + dma(2, n.comps, n.mode)
         + dma(n.group) + dma(n.zs) + dma(n.group) + dma(n.comps, n.x),
         compiler_params=pltpu.CompilerParams(
-            collective_id=1, has_side_effects=True, vmem_limit_bytes=48 << 20
+            collective_id=1, has_side_effects=True, vmem_limit_bytes=62 << 20
         ),
         name="ritz",
-    )(y0, cls, table, coef_t)
+    )(modes_in, class_map, table, coefficients)
 
 
 def per_device(n, modes_in, class_map, stiffness_table, coefficients):
-    y0 = jnp.transpose(modes_in[:, :, 0], (1, 2, 0, 3))
-    width = n.x * n.own
-    start = lax.div(lax.axis_index("mode"), n.x) * width
-    coef_t = lax.dynamic_slice_in_dim(coefficients.T, start, width, 0)
-    result = run(n, y0, class_map[0], stiffness_table, coef_t)
+    result = run(n, modes_in[:, :, 0], class_map[0], stiffness_table, coefficients)
     return jnp.transpose(result, (2, 0, 1, 3))[:, :, None]
 
 

time: 110 us -> 107 us (0.973)
  local copies, waits for them, and re-layouts: 3.66 us -> 1.84 us
    unnamed x8 -> x0, local copies, waits for them, and re-layouts: 2.74 us -> none
where the time goes in v3:
time: 107 us
  Pallas kernels  105 us (98%)
  local copies, waits for them, and re-layouts  1.84 us (2%)
    pallas_call x1, Pallas kernels, run(): pl.pallas_call(functools.partial(kernel, n), out_shape=jax.ShapeDtypeStru...  105 us

profile of v3, /device:TPU:1, one launch (start us, length us, event | category | flops | bytes accessed | tf_op | source)
XLA Modules:
  0.0 107.0 jit_solution(2041025162567240210)
XLA Ops:
  0.0 105.2 %ritz.1 = bf16[3,32,16,128]{3,2,1,0:T(8,128)(2,1)} custom-call(bf16[16,3,32,128]{3,2,1,0:T(8,128)(2,1)} %bitcast.6, s32[32,128]{1,0:T(8,128)} %bitcast.7, f32[8]{0:T(128)} %table_hbm.1, f32[128,128]{1,0:T(8,128)} %coef_hbm.1), custom_call_target="tpu_custom_call" | custom-call | tf_op jit(solution)/shard_map/ritz/pallas_call | solution.py:389
  105.2 1.8 %copy.5 = bf16[16,3,1,32,128]{4,3,2,1,0:T(8,128)(2,1)} copy(bf16[16,3,1,32,128]{4,0,3,1,2:T(8,128)(2,1)} %bitcast.5) | data formatting | bytes 786432 | tf_op jit(solution)/shard_map/broadcast_in_dim | solution.py:431

commit v4 on v3

--- a/solution.py
+++ b/solution.py
@@ -255,17 +255,20 @@
                 filt[c, at] = ((value + value) - y1[c, at]).astype(BF16)
         leave(1)
 
-    mine = pl.ds(pl.multiple_of(me.m * n.own, n.own), n.own)
-
     def share(c, d, part):
-        to = lax.rem(me.m + d, n.mode)
-        to_x, to_zh = lax.rem(to, n.x), lax.div(to, n.x)
-        at = lax.rem(to_zh + part, n.z_hi) * n.half
-        src = filt.at[c, pl.ds(to_x * n.rows + at, n.half)]
-        dst = block.at[c, pl.ds(at, n.half), mine]
-        return remote(src, dst, asend.at[part, c, d], arecv.at[part, c, d], {"mode": to})
-
-    shares = range(1, n.mode)
+        dz, dx = divmod(d, n.x)
+        to_zh, to_x = lax.rem(me.zh + dz, n.z_hi), lax.rem(me.x + dx, n.x)
+        at, count = (0, n.rows) if dz == 0 else (lax.rem(to_zh + part, n.z_hi) * n.half, n.half)
+        src = filt.at[c, pl.ds(to_x * n.rows + at, count)]
+        dst = block.at[c, me.m, pl.ds(at, count)]
+        to = {"mode": to_zh * n.x + to_x}
+        return remote(src, dst, asend.at[part, c, d], arecv.at[part, c, d], to)
+
+    def every_mode(c, k):
+        return jnp.concatenate([block[c, i, k] for i in range(n.mode)])
+
+    others = list(range(n.x, n.mode))
+    shares = others + list(range(1, n.x))
     for r in range(3):
         for c in range(n.comps):
             def arrive(p):
@@ -281,16 +284,13 @@
             if r == 2:
                 for d in shares:
                     share(c, d, 0).start()
-                block[c, :, mine, :] = filt[c, pl.ds(me.x * n.rows, n.rows)]
-    for d in shares:
-        share(0, d, 1).start()
-
+                block[c, me.m] = filt[c, pl.ds(me.x * n.rows, n.rows)]
     product = jnp.zeros((n.modes, n.modes), F32)
     for c in range(n.comps):
         for d in shares:
             share(c, d, 0).wait_recv()
         for k in range(n.half):
-            a = block[c, me.zh * n.half + k]
+            a = every_mode(c, me.zh * n.half + k)
             product = product + lax.dot_general(
                 a, a, (((1,), (1,)), ((), ())), preferred_element_type=F32
             )
@@ -311,6 +311,8 @@
 
     for i in range(len(steps)):
         scatter(i).start()
+    for d in others:
+        share(0, d, 1).start()
     piece = own[me.g]
     for i in range(len(steps)):
         scatter(i).wait_recv()
@@ -329,7 +331,7 @@
     for i in range(len(steps)):
         gather(i).start()
     for c in range(1, n.comps):
-        for d in shares:
+        for d in others:
             share(c, d, 1).start()
     for i in range(len(steps)):
         gather(i).wait_recv()
@@ -348,19 +350,20 @@
 
     def back(c, d):
         to = lax.rem(me.x + d, n.x)
-        src = held.at[c, :, pl.ds(pl.multiple_of(to * n.own, n.own), n.own)]
+        src = held.at[c, to]
         dst = out.at[c, pl.ds(me.x * n.rows, n.rows)]
         return remote(src, dst, send4.at[c, d], recv4.at[c, d], {"mode": me.zh * n.x + to})
 
-    kept = pl.ds(pl.multiple_of(me.x * n.own, n.own), n.own)
-    for c in range(n.comps):
-        for d in shares:
+    for c in range(n.comps):
+        for d in others:
             share(c, d, 1).wait_recv()
         for k in range(n.rows):
-            held[c, k] = jnp.dot(mix_t, block[c, k], preferred_element_type=F32).astype(BF16)
+            turned = jnp.dot(mix_t, every_mode(c, k), preferred_element_type=F32).astype(BF16)
+            for q in range(n.x):
+                held[c, q, k] = turned[q * n.own : (q + 1) * n.own]
         for d in range(1, n.x):
             back(c, d).start()
-        out[c, pl.ds(me.x * n.rows, n.rows)] = held[c, :, kept, :]
+        out[c, pl.ds(me.x * n.rows, n.rows)] = held[c, me.x]
 
     for c in range(n.comps):
         for r in range(3):
@@ -369,6 +372,7 @@
                     hop(r, c, d, p).wait_send()
         for d in shares:
             share(c, d, 0).wait_send()
+        for d in others:
             share(c, d, 1).wait_send()
     for i in range(len(steps)):
         scatter(i).wait_send()
@@ -407,7 +411,7 @@
         + [pltpu.VMEM(plane, F32)] * 2
         + [pltpu.VMEM(plane, BF16)] * 3
         + [
-            pltpu.VMEM((n.comps, n.rows, n.modes, n.ny), BF16),
+            pltpu.VMEM((n.comps, n.mode, n.rows, n.own, n.ny), BF16),
             pltpu.VMEM((n.group,) + piece, F32),
             pltpu.VMEM((n.group,) + piece, F32),
             pltpu.VMEM((n.zs + 1,) + piece, F32),
@@ -415,7 +419,7 @@
             pltpu.VMEM((n.group,) + piece, F32),
             pltpu.VMEM(square, F32),
             pltpu.VMEM(square, F32),
-            pltpu.VMEM((n.comps, n.rows, n.x * n.own, n.ny), BF16),
+            pltpu.VMEM((n.comps, n.x, n.rows, n.own, n.ny), BF16),
         ]
         + dma(3, 2, n.comps, 2) + dma(2) + dma(2, n.comps, n.mode)
         + dma(n.group) + dma(n.zs) + dma(n.group) + dma(n.comps, n.x),

time: 107 us -> 105 us (0.981); the launches traced: 107 us -> 104 us
  Pallas kernels: 105 us -> 102 us
    pallas_call x1, Pallas kernels: 105 us -> 102 us  [run(): pl.pallas_call(functools.partial(kernel, n), out_shape=jax.ShapeDtypeStru...]
where the time goes in v4:
time: 105 us; the launch traced here: 104 us
  Pallas kernels  102 us (97%)
  local copies, waits for them, and re-layouts  1.84 us (2%)
    pallas_call x1, Pallas kernels, run(): pl.pallas_call(functools.partial(kernel, n), out_shape=jax.ShapeDtypeStru...  102 us

profile of v4, /device:TPU:1, one launch (start us, length us, event | category | flops | bytes accessed | tf_op | source)
XLA Modules:
  0.0 103.7 jit_solution(5153379548576863936)
XLA Ops:
  0.0 101.9 %ritz.1 = bf16[3,32,16,128]{3,2,1,0:T(8,128)(2,1)} custom-call(bf16[16,3,32,128]{3,2,1,0:T(8,128)(2,1)} %bitcast.6, s32[32,128]{1,0:T(8,128)} %bitcast.7, f32[8]{0:T(128)} %table_hbm.1, f32[128,128]{1,0:T(8,128)} %coef_hbm.1), custom_call_target="tpu_custom_call" | custom-call | tf_op jit(solution)/shard_map/ritz/pallas_call | solution.py:393
  101.9 1.8 %copy.5 = bf16[16,3,1,32,128]{4,3,2,1,0:T(8,128)(2,1)} copy(bf16[16,3,1,32,128]{4,0,3,1,2:T(8,128)(2,1)} %bitcast.5) | data formatting | bytes 786432 | tf_op jit(solution)/shard_map/broadcast_in_dim | solution.py:435

commit v5 on v4

--- a/solution.py
+++ b/solution.py
@@ -107,6 +107,18 @@
     steps = sorted(steps[1:], key=lambda s: (-far(s[0], n.x) - far(s[1], n.y), s))
     climbs = sorted(range(1, n.zs), key=lambda d: (-far(d, n.zs), d))
 
+    barrier = pltpu.get_barrier_semaphore()
+    friends = [nxt, prv]
+    friends += [me.in_column(lax.rem(me.z + d, n.zs)) for d in climbs]
+    for dz in range(1, n.z_hi):
+        for dx in range(1, n.x):
+            friends.append({
+                "mode": lax.rem(me.zh + dz, n.z_hi) * n.x + lax.rem(me.x + dx, n.x)
+            })
+    friends += [me.in_group(*step)[0] for step in steps]
+    for device in friends:
+        pl.semaphore_signal(barrier, inc=1, device_id=device, device_id_type=MESH)
+
     loads = [
         pltpu.make_async_copy(cls_hbm, cls, loaded.at[0]),
         pltpu.make_async_copy(table_hbm, table, loaded.at[1]),
@@ -118,18 +130,6 @@
     ]
     for load in loads:
         load.start()
-
-    barrier = pltpu.get_barrier_semaphore()
-    friends = [nxt, prv]
-    friends += [me.in_group(*step)[0] for step in steps]
-    friends += [me.in_column(lax.rem(me.z + d, n.zs)) for d in climbs]
-    for dz in range(1, n.z_hi):
-        for dx in range(1, n.x):
-            friends.append({
-                "mode": lax.rem(me.zh + dz, n.z_hi) * n.x + lax.rem(me.x + dx, n.x)
-            })
-    for device in friends:
-        pl.semaphore_signal(barrier, inc=1, device_id=device, device_id_type=MESH)
 
     size = n.own * n.own
     at_row = lax.broadcasted_iota(jnp.int32, (size, size), 0)

time: 105 us -> 104 us (level)
  the two profiles are of different devices: /device:TPU:1 before, /device:TPU:32 now
where the time goes in v5:
time: 104 us
  Pallas kernels  102 us (98%)
  local copies, waits for them, and re-layouts  1.84 us (2%)
    pallas_call x1, Pallas kernels, run(): pl.pallas_call(functools.partial(kernel, n), out_shape=jax.ShapeDtypeStru...  102 us

profile of v5, /device:TPU:32, one launch (start us, length us, event | category | flops | bytes accessed | tf_op | source)
XLA Modules:
  0.0 103.9 jit_solution(7765068032014233261)
XLA Ops:
  0.0 102.1 %ritz.1 = bf16[3,32,16,128]{3,2,1,0:T(8,128)(2,1)} custom-call(bf16[16,3,32,128]{3,2,1,0:T(8,128)(2,1)} %bitcast.6, s32[32,128]{1,0:T(8,128)} %bitcast.7, f32[8]{0:T(128)} %table_hbm.1, f32[128,128]{1,0:T(8,128)} %coef_hbm.1), custom_call_target="tpu_custom_call" | custom-call | tf_op jit(solution)/shard_map/ritz/pallas_call | solution.py:393
  102.1 1.8 %copy.5 = bf16[16,3,1,32,128]{4,3,2,1,0:T(8,128)(2,1)} copy(bf16[16,3,1,32,128]{4,0,3,1,2:T(8,128)(2,1)} %bitcast.5) | data formatting | bytes 786432 | tf_op jit(solution)/shard_map/broadcast_in_dim | solution.py:435
